TPU v7x, 32 devices: a whole 2x2x4 slice. The times are simulated.
32 devices in a mesh: groups: 2 (over x), expert: 16 (over z, y, core).
Axes of the slice: x: 2, y: 2, z: 4, core: 2. Of those that a mesh axis runs over, the one named last changes fastest.
Arguments:
- tokens: bfloat16 [4096, 4096], P(('groups', 'expert')), parts along dimension 0, may hold values from -6 to 6
- routes: int32 [4096, 4], P(('groups', 'expert')), parts along dimension 0, may hold values from 0 to 7, all different within a row; in each aligned block of 128 rows (0 to 127, 128 to 255, ...) at most 64 rows name the same one
- route_weights: float32 [4096, 4], P(('groups', 'expert')), parts along dimension 0, may hold values from 0.1 to 1
- gate_weight: bfloat16 [4096, 7168], P(None, 'expert'), may hold values from -0.09375 to 0.09375
- up_weight: bfloat16 [4096, 7168], P(None, 'expert'), may hold values from -0.09375 to 0.09375
- down_weight: bfloat16 [896, 32768], P(None, 'expert'), may hold values from -0.1875 to 0.1875
Outputs:
- mixed: bfloat16 [4096, 4096], P(('groups', 'expert')), parts along dimension 0
There are 2 independent parts, one for each index of `groups`. A program takes and returns all parts, laid end to end along the dimension named above; an argument that names none is the same for every part. Nothing has to cross between parts.
Inputs may be any that keep to these rules, and one draw needn't show every extreme that they name: `routes`: each row names 4 different experts; in each aligned block of 128 rows (the rows of one device) every expert is named by exactly 64 rows.
All inputs are finite; a program needn't handle non-finite values.
Results may differ from a plain program's by a relative error of at most 0.008.
Values may be sent and summed in bfloat16 or wider, within the bound.
No kernel may reach another device: no remote copies, remote signals or barrier semaphores. Data moves between devices by JAX's collectives and lax.ppermute only.
A program may use at most 128 MiB of HBM per device.

v0:
```python
import jax
import jax.numpy as jnp
from jax import lax
from jax.sharding import PartitionSpec as P


def swapped(x, axis, apart):
    return lax.ppermute(x, axis, [(i, i ^ 1 << apart) for i in range(lax.axis_size(axis))])


def expert_hidden(rows, gate_part, up_part, parity):
    gate = jnp.dot(rows, gate_part, preferred_element_type=jnp.float32)
    upval = jnp.dot(rows, up_part, preferred_element_type=jnp.float32)
    hidden = (jax.nn.silu(gate) * upval).astype(jnp.bfloat16)
    partner = swapped(hidden, "expert", 0)
    return jnp.where(
        parity == 0, jnp.concatenate([hidden, partner], 1), jnp.concatenate([partner, hidden], 1)
    )


def shards(tokens, routes, route_weights, gate_weight, up_weight, down_weight):
    tok_rows, top_count = routes.shape
    width = tokens.shape[1]
    half_width = down_weight.shape[1]
    devices = lax.axis_size("expert")
    experts = devices // 2
    capacity = tok_rows * top_count // experts
    parity = lax.axis_index("expert") % 2
    flat = routes.reshape(-1)
    onehot = (flat[:, None] == jnp.arange(experts, dtype=jnp.int32)[None, :]).astype(jnp.int32)
    before = jnp.cumsum(onehot, axis=0) - onehot
    slot_of = jnp.sum(before * onehot, axis=1)
    position = flat * capacity + slot_of
    assign_ids = jnp.arange(flat.shape[0], dtype=jnp.int32) // top_count
    owner = jnp.zeros((experts * capacity,), jnp.int32).at[position].set(assign_ids)
    gathered = tokens[owner]
    outgoing = jnp.broadcast_to(
        gathered.reshape(experts, 1, capacity, width), (experts, 2, capacity, width)
    )
    outgoing = outgoing.reshape(devices, capacity, width)
    received = lax.all_to_all(outgoing, "expert", split_axis=0, concat_axis=0, tiled=True)
    count, items, _ = received.shape
    hidden = expert_hidden(received.reshape(count * items, width), gate_weight, up_weight, parity)
    produced = jnp.dot(hidden, down_weight, preferred_element_type=jnp.float32).astype(jnp.bfloat16)
    returned = lax.all_to_all(
        produced.reshape(count, items, half_width),
        "expert",
        split_axis=0,
        concat_axis=0,
        tiled=True,
    )
    returned = returned.reshape(experts, 2, capacity, half_width).transpose(0, 2, 1, 3)
    expert_rows = returned.reshape(experts * capacity, width)
    picked = expert_rows[position].reshape(tok_rows, top_count, width)
    mixed = jnp.einsum("tk,tkd->td", route_weights, picked.astype(jnp.float32))
    return mixed.astype(jnp.bfloat16)


def solution(mesh):
    return jax.shard_map(
        shards,
        mesh=mesh,
        in_specs=(
            P(("groups", "expert"), None),
            P(("groups", "expert"), None),
            P(("groups", "expert"), None),
            P(None, "expert"),
            P(None, "expert"),
            P(None, "expert"),
        ),
        out_specs=P(("groups", "expert"), None),
        check_vma=False,
    )
```

profile of v0, /device:TPU:15, one launch (start us, length us, event | category | flops | bytes accessed | tf_op | source)
XLA Modules:
  0.0 359.2 jit_solution(6796952720300360334)
XLA Ops:
  0.0 0.0 copy-start
  0.0 0.8 broadcast_multiply_fusion
  0.8 0.8 copy.9
  1.6 0.1 eq.35
  1.7 0.1 eq.31
  1.8 0.1 copy.8
  1.9 0.1 mul.28
  2.0 1.1 reduce-window.6
  3.2 0.2 slice_reduce_fusion
  3.4 0.1 fusion.7
  3.5 2.4 scatter_custom_fusion
  6.0 0.0 copy-done
  6.0 4.4 %gather_fusion = bf16[512,4096]{1,0:T(8,128)(2,1)} fusion(bf16[128,4096]{1,0:T(8,128)(2,1)S(1)} %copy-done, s32[1024]{0:T(1024)S(1)} %pad_clamp_fusion.1), kind=kCustom, calls=%fused_computation | custom fusion | bytes 8390656 | tf_op jit(solution)/shard_map/gather | solution.py:36
  10.4 6.5 %broadcast_in_dim.15 = bf16[8,2,64,4096]{3,2,1,0:T(8,128)(2,1)} broadcast(bf16[8,64,4096]{2,1,0:T(8,128)(2,1)} %bitcast.32), dimensions={0,2,3} | broadcast | bytes 12582912 | tf_op jit(solution)/shard_map/broadcast_in_dim | solution.py:37
  16.9 188.9 %all_to_all.10 = bf16[16,64,4096]{2,1,0:T(8,128)(2,1)S(1)} all-to-all(bf16[16,64,4096]{2,1,0:T(8,128)(2,1)} %bitcast.31), channel_id=1, replica_groups=mesh['groups'=2,'expert'=16] {'expert'}, dimensions={0} | all-to-all | bytes 16777216 | tf_op jit(solution)/shard_map/all_to_all | solution.py:41
  205.8 0.0 copy-done.2
  205.8 4.0 %fusion.15 = f32[1024,448]{0,1:T(8,128)S(1)} fusion(bf16[1024,4096]{1,0:T(8,128)(2,1)S(1)} %bitcast.34, bf16[4096,448]{0,1:T(8,128)(2,1)S(1)} %copy-done.2), kind=kOutput, calls=%fused_computation.35 | convolution fusion | flops 3758096384 | bytes 13893632 | tf_op jit(solution)/shard_map/dot_general | solution.py:12
  209.8 0.0 copy-done.3
  209.8 4.2 %multiply_convert_fusion = bf16[1024,448]{0,1:T(8,128)(2,1)S(1)} fusion(f32[1024,448]{0,1:T(8,128)S(1)} %fusion.15, bf16[1024,4096]{1,0:T(8,128)(2,1)S(1)} %bitcast.35, bf16[4096,448]{0,1:T(8,128)(2,1)S(1)} %copy-done.3), kind=kOutput, calls=%fused_computation.11 | convolution fusion | flops 3760848896 | bytes 14811136 | tf_op jit(solution)/shard_map/dot_general | solution.py:13
  214.0 0.3 collective-permute-start
  214.3 2.3 collective-permute-done
  216.5 8.4 %convolution_convert_fusion = bf16[1024,2048]{1,0:T(8,128)(2,1)} fusion(bf16[896,2048]{1,0:T(8,128)(2,1)} %param.11, bf16[1024,448]{0,1:T(8,128)(2,1)S(1)} %collective-permute-done, bf16[1024,448]{0,1:T(8,128)(2,1)S(1)} %multiply_convert_fusion, pred[]{:T(512)S(6)} %eq.30), kind=kOutput, calls=%fused_computation.3 | convolution fusion | flops 3768451072 | bytes 9699329 | tf_op jit(solution)/shard_map/dot_general | solution.py:44
  224.9 5.8 %all-to-all-start.1 = ((bf16[16,64,2048]{2,1,0:T(8,128)(2,1)}), bf16[16,64,2048]{2,1,0:T(8,128)(2,1)}, u32[]{:S(2)}, u32[]{:S(2)}) async-start(bf16[16,64,2048]{2,1,0:T(8,128)(2,1)} %bitcast.36), calls=%async_computation.1 | async-start | bytes 8388608 | tf_op jit(solution)/shard_map/all_to_all | solution.py:45
  230.7 0.0 copy-done.1
  230.7 0.2 copy.12
  230.9 92.3 %all-to-all-done.1 = bf16[16,64,2048]{2,1,0:T(8,128)(2,1)} async-done(((bf16[16,64,2048]{2,1,0:T(8,128)(2,1)}), bf16[16,64,2048]{2,1,0:T(8,128)(2,1)}, u32[]{:S(2)}, u32[]{:S(2)}) %all-to-all-start.1) | async-done | bytes 4194336 | tf_op jit(solution)/shard_map/all_to_all | solution.py:45
  323.2 6.5 %copy.11 = bf16[8,2,64,2048]{3,1,2,0:T(2,128)(2,1)S(1)} copy(bf16[8,2,64,2048]{3,2,1,0:T(8,128)(2,1)} %bitcast.8) | data formatting | bytes 8388608 | tf_op jit(solution)/shard_map/reshape | solution.py:52
  329.7 4.4 %copy.14 = bf16[64,8,2,2048]{3,1,2,0:T(8,128)(2,1)} copy(bf16[64,8,2,2048]{3,2,1,0:T(2,128)(2,1)S(1)} %bitcast.33) | data formatting | bytes 8388608
  334.1 11.3 %gather_fusion.1 = bf16[512,4096]{1,0:T(8,128)(2,1)} fusion(bf16[512,4096]{1,0:T(8,128)(2,1)} %bitcast.30, s32[1024]{0:T(1024)S(1)} %pad_clamp_fusion), kind=kCustom, calls=%fused_computation.1 | custom fusion | bytes 8390656 | tf_op jit(solution)/shard_map/gather | solution.py:54
  345.4 7.2 %reshape.72 = bf16[128,4,4096]{2,1,0:T(4,128)(2,1)} reshape(bf16[512,4096]{1,0:T(8,128)(2,1)} %gather_fusion.1) | data formatting | bytes 8388608 | tf_op jit(solution)/shard_map/reshape | solution.py:54
  352.6 4.5 %fusion.16 = bf16[128,1,4096]{2,1,0:T(2,128)(2,1)S(1)} fusion(bf16[128,4,4096]{2,1,0:T(4,128)(2,1)} %reshape.72, bf16[128,4,1]{1,2,0:T(2,128)(2,1)S(1)} %copy.12), kind=kOutput, calls=%fused_computation.36 | convolution fusion | flops 4194304 | bytes 5243904 | tf_op jit(solution)/shard_map/tk,tkd->td/dot_general | solution.py:55
  357.1 2.1 copy.16
  (11 shorter events, 0.1 us)
Async XLA Ops:
  0.0 6.0 %copy-start = (bf16[128,4096]{1,0:T(8,128)(2,1)S(1)}, bf16[128,4096]{1,0:T(8,128)(2,1)}, u32[]{:S(2)}) copy-start(bf16[128,4096]{1,0:T(8,128)(2,1)} %param.6) | copy-start | bytes 3145732
  16.9 188.9 %copy-start.2 = (bf16[4096,448]{0,1:T(8,128)(2,1)S(1)}, bf16[4096,448]{0,1:T(8,128)(2,1)}, u32[]{:S(2)}) copy-start(bf16[4096,448]{0,1:T(8,128)(2,1)} %param.9) | copy-start | bytes 11010052
  205.8 4.0 %copy-start.3 = (bf16[4096,448]{0,1:T(8,128)(2,1)S(1)}, bf16[4096,448]{0,1:T(8,128)(2,1)}, u32[]{:S(2)}) copy-start(bf16[4096,448]{0,1:T(8,128)(2,1)} %param.10) | copy-start | bytes 11010052
  214.0 2.5 collective-permute-start
  224.9 5.8 %copy-start.1 = (f32[128,4]{0,1:T(4,128)S(1)}, f32[128,4]{0,1:T(4,128)}, u32[]{:S(2)}) copy-start(f32[128,4]{0,1:T(4,128)} %param.8) | copy-start | bytes 6148
  224.9 98.3 %all-to-all-start.1 = ((bf16[16,64,2048]{2,1,0:T(8,128)(2,1)}), bf16[16,64,2048]{2,1,0:T(8,128)(2,1)}, u32[]{:S(2)}, u32[]{:S(2)}) async-start(bf16[16,64,2048]{2,1,0:T(8,128)(2,1)} %bitcast.36), calls=%async_computation.1 | async-start | bytes 8388608 | tf_op jit(solution)/shard_map/all_to_all | solution.py:45
where the time goes:
time: 360 us; the launch traced here: 359 us
  blocking collectives  189 us (52%)
  waiting for transfers between devices  94.5 us (26%)
  local copies, waits for them, and re-layouts  46.3 us (13%)
  matrix products  21 us (6%)
  starting transfers between devices  6.11 us (2%)
    all_to_all x1, blocking collectives, shards(): lax.all_to_all(outgoing, 'expert', split_axis=0, concat_axis=0, tiled=True)  189 us
    all_to_all x1, waiting for transfers between devices, shards(): lax.all_to_all(produced.reshape(count, items, half_width), 'expert', spli...  92.3 us
    gather x1, local copies, waits for them, and re-layouts, shards(): picked = expert_rows[position].reshape(tok_rows, top_count, width)  11.3 us
    dot_general x1, matrix products, shards(): jnp.dot(hidden, down_weight, preferred_element_type=jnp.float32)  8.37 us
  transfers between devices with their start and end apart: 2, of which 2 were waited for; matrix products, arithmetic and copies ran while one was open for 0% of the time, Pallas kernels for 0%

commit v1 on v0

--- a/solution.py
+++ b/solution.py
@@ -1,16 +1,28 @@
+import functools
+
 import jax
+import jax.experimental.pallas as pl
+import jax.experimental.pallas.tpu as pltpu
 import jax.numpy as jnp
 from jax import lax
 from jax.sharding import PartitionSpec as P
 
+CHUNKS = 1
+CROSS_ROWS = 40
+LANES = 128
+
 
 def swapped(x, axis, apart):
     return lax.ppermute(x, axis, [(i, i ^ 1 << apart) for i in range(lax.axis_size(axis))])
 
 
+def dot32(a, b):
+    return jnp.dot(a, b, preferred_element_type=jnp.float32)
+
+
 def expert_hidden(rows, gate_part, up_part, parity):
-    gate = jnp.dot(rows, gate_part, preferred_element_type=jnp.float32)
-    upval = jnp.dot(rows, up_part, preferred_element_type=jnp.float32)
+    gate = dot32(rows, gate_part)
+    upval = dot32(rows, up_part)
     hidden = (jax.nn.silu(gate) * upval).astype(jnp.bfloat16)
     partner = swapped(hidden, "expert", 0)
     return jnp.where(
@@ -18,7 +30,7 @@
     )
 
 
-def shards(tokens, routes, route_weights, gate_weight, up_weight, down_weight):
+def dispatched(tokens, routes, route_weights, gate_weight, up_weight, down_weight):
     tok_rows, top_count = routes.shape
     width = tokens.shape[1]
     half_width = down_weight.shape[1]
@@ -41,7 +53,7 @@
     received = lax.all_to_all(outgoing, "expert", split_axis=0, concat_axis=0, tiled=True)
     count, items, _ = received.shape
     hidden = expert_hidden(received.reshape(count * items, width), gate_weight, up_weight, parity)
-    produced = jnp.dot(hidden, down_weight, preferred_element_type=jnp.float32).astype(jnp.bfloat16)
+    produced = dot32(hidden, down_weight).astype(jnp.bfloat16)
     returned = lax.all_to_all(
         produced.reshape(count, items, half_width),
         "expert",
@@ -56,9 +68,271 @@
     return mixed.astype(jnp.bfloat16)
 
 
+def along_line(x, pairs):
+    moves = [((a * 2 + s) * 2 + c, (b * 2 + s) * 2 + c) for a, b in pairs for s in (0, 1) for c in (0, 1)]
+    return lax.ppermute(x, "expert", moves)
+
+
+def exchange_outer(x):
+    return along_line(x, [(0, 1), (1, 0), (2, 3), (3, 2)])
+
+
+def exchange_middle(x):
+    return along_line(x, [(1, 2), (2, 1)])
+
+
+def move_out(x):
+    return along_line(x, [(1, 0), (2, 3)])
+
+
+def move_in(x):
+    return along_line(x, [(0, 1), (3, 2)])
+
+
+def contract(a, b, da, db):
+    return lax.dot_general(a, b, (((da,), (db,)), ((), ())), preferred_element_type=jnp.float32)
+
+
+def iota(shape, dim):
+    return lax.broadcasted_iota(jnp.int32, shape, dim)
+
+
+def eye(n):
+    return (iota((n, n), 0) == iota((n, n), 1)).astype(jnp.bfloat16)
+
+
+def scale_of(ext, expert, experts):
+    lane = iota(ext.shape, 1)
+    mine = (lane % experts == expert) & (lane < 3 * experts)
+    return jnp.sum(jnp.where(mine, ext.astype(jnp.float32), 0.0), axis=1, keepdims=True)
+
+
+def prepare_kernel(experts, idx, tokens, routes, weights, *outs):
+    rows, width = tokens.shape
+    chunks = len(outs) - 1 if len(outs) > 1 else 1
+    lane = iota((rows, LANES), 1)
+    part = lane // experts
+    full = jnp.zeros((rows, LANES), jnp.float32)
+    for k in range(routes.shape[1]):
+        full += jnp.where(lane % experts == routes[:, k : k + 1], weights[:, k : k + 1], 0.0)
+    high = full.astype(jnp.bfloat16).astype(jnp.float32)
+    mid = (full - high).astype(jnp.bfloat16).astype(jnp.float32)
+    low = full - high - mid
+    ext = jnp.where(part == 0, high, jnp.where(part == 1, mid, jnp.where(part == 2, low, 0.0)))
+    ext = ext.astype(jnp.bfloat16)
+    if chunks == 1:
+        outs[0][:, :width] = tokens[...]
+        outs[0][:, width:] = ext
+        return
+    gray = jnp.zeros((rows, 1), jnp.int32)
+    bit = jnp.zeros((rows, 1), jnp.int32)
+    for z in range(experts // 2):
+        named = jnp.zeros((rows, 1), jnp.int32)
+        for k in range(routes.shape[1]):
+            named += (routes[:, k : k + 1] == idx[5] + 2 * z).astype(jnp.int32)
+        bit = bit ^ named
+        gray = gray * 2 + bit
+    down = jnp.broadcast_to(gray.astype(jnp.float32), (rows, rows))
+    across = contract(down.astype(jnp.bfloat16), eye(rows), 0, 0)
+    first, second = iota((rows, rows), 0), iota((rows, rows), 1)
+    ahead = (down < across) | ((down == across) & (first < second))
+    rank = jnp.sum(ahead.astype(jnp.float32), axis=0, keepdims=True).astype(jnp.int32)
+    size = rows // chunks
+    target = rank % chunks * size + rank // chunks
+    order = (first == target).astype(jnp.bfloat16)
+    outs[-1][...] = order
+    ext = dot32(order, ext).astype(jnp.bfloat16)
+    for q in range(chunks):
+        outs[q][:, width:] = ext[q * size : (q + 1) * size]
+    step = 1024
+    for n in range(0, width, step):
+        moved = dot32(order, tokens[:, n : n + step]).astype(jnp.bfloat16)
+        for q in range(chunks):
+            outs[q][:, n : n + step] = moved[q * size : (q + 1) * size]
+
+
+def pick_kernel(experts, dense, idx, *refs):
+    *blocks, own_out, cross_out, pick_out = refs
+    rows, total = blocks[0].shape
+    own_rows, cross_rows = own_out.shape[0], cross_out.shape[0]
+    inner = idx[3] == 1
+
+    def load(cols):
+        x = blocks[0][:, cols]
+        return jnp.where(inner, x, blocks[1][:, cols]) if len(blocks) > 1 else x
+
+    ext = load(slice(total - LANES, total))
+
+    def picks(expert, count):
+        mask = jnp.broadcast_to(scale_of(ext, expert, experts) > 0, (rows, LANES)).astype(jnp.bfloat16)
+        upto = (iota((rows, rows), 0) <= iota((rows, rows), 1)).astype(jnp.bfloat16)
+        place = contract(mask, upto, 0, 0)[:count]
+        named = contract(mask, eye(rows), 0, 0)[:count]
+        slot = iota((count, rows), 0).astype(jnp.float32)
+        return ((named > 0.5) & (place - 1.0 == slot)).astype(jnp.float32)
+
+    own = eye(rows).astype(jnp.float32) if dense else picks(idx[1], own_rows)
+    pick = jnp.concatenate([own, picks(idx[2], cross_rows)], 0).astype(jnp.bfloat16)
+    pick_out[...] = pick
+    step = total // 3
+    for n in range(0, total, step):
+        got = dot32(pick, load(slice(n, n + step)))
+        own_out[:, n : n + step] = got[:own_rows].astype(jnp.bfloat16)
+        cross_out[:, n : n + step] = got[own_rows:].astype(jnp.bfloat16)
+
+
+def expert_kernel(experts, idx, own, cross, ga, gb, ua, ub, da, db, own_out, cross_out, hidden):
+    own_rows, total = own.shape
+    width = total - LANES
+    core, expert = idx[0], idx[1]
+    half = ga.shape[0]
+    x = jnp.concatenate([own[:, :width], cross[:, :width]], 0)
+    ext = jnp.concatenate([own[:, width:], cross[:, width:]], 0)
+    scale = scale_of(ext, expert, experts)
+    for place, g, u in ((core, ga, ua), (1 - core, gb, ub)):
+        gate = contract(x, g[...], 1, 1)
+        upval = contract(x, u[...], 1, 1)
+        hidden[place] = (gate / (1.0 + jnp.exp(-gate)) * upval * scale).astype(jnp.bfloat16)
+    step = 512
+    cols = da.shape[1]
+    for n in range(0, 2 * cols, step):
+        d, m = (da, n) if n < cols else (db, n - cols)
+        made = dot32(hidden[0], d[:half, m : m + step]) + dot32(hidden[1], d[half:, m : m + step])
+        own_out[:, n : n + step] = made[:own_rows].astype(jnp.bfloat16)
+        cross_out[:, n : n + step] = made[own_rows:].astype(jnp.bfloat16)
+
+
+def combine_kernel(placed, idx, pick, own, cross, *refs):
+    *more, out = refs
+    width = own.shape[1]
+    step = 1024
+    for n in range(0, width, step):
+        cols = slice(n, n + step)
+        got = contract(pick[...], jnp.concatenate([own[:, cols], cross[:, cols]], 0), 0, 0)
+        for ref in more:
+            got += ref[:, cols].astype(jnp.float32)
+        start = pl.multiple_of((idx[4] + n) % width, step) if placed else n
+        out[:, pl.ds(start, step)] = got.astype(jnp.bfloat16)
+
+
+def place_kernel(idx, order, *refs):
+    *chunks, out = refs
+    width = out.shape[1]
+    step = 1024
+    for n in range(0, width, step):
+        cols = slice(n, n + step)
+        got = contract(order[...], jnp.concatenate([c[:, cols] for c in chunks], 0), 0, 0)
+        out[:, pl.ds(pl.multiple_of((idx[4] + n) % width, step), step)] = got.astype(jnp.bfloat16)
+
+
+def call(kernel, outs, idx, *args, scratch=(), flops=0, limit=24):
+    vmem = pl.BlockSpec(memory_space=pltpu.VMEM)
+    size = sum(a.size * a.dtype.itemsize for a in list(args) + list(outs))
+    return pl.pallas_call(
+        kernel,
+        out_shape=outs,
+        in_specs=[pl.BlockSpec(memory_space=pltpu.SMEM)] + [vmem] * len(args),
+        out_specs=[vmem] * len(outs),
+        scratch_shapes=list(scratch),
+        compiler_params=pltpu.CompilerParams(vmem_limit_bytes=limit << 20),
+        cost_estimate=pl.CostEstimate(flops=flops, bytes_accessed=size, transcendentals=0),
+    )(idx, *args)
+
+
+def lined(tokens, routes, route_weights, gate_weight, up_weight, down_weight):
+    tok_rows, top_count = routes.shape
+    width = tokens.shape[1]
+    devices = lax.axis_size("expert")
+    experts = devices // 2
+    capacity = tok_rows * top_count // experts
+    half = gate_weight.shape[1]
+    index = lax.axis_index("expert")
+    core, side, line = index % 2, index // 2 % 2, index // 4
+    inner = ((line == 1) | (line == 2)).astype(jnp.int32)
+    idx = jnp.stack(
+        [core, 2 * line + side, 2 * line + 1 - side, inner, core * down_weight.shape[1], 1 - side]
+    ).astype(jnp.int32)
+    rows = tok_rows // CHUNKS
+    dense = CHUNKS > 1
+    own_rows = rows if dense else capacity
+    cross_rows = CROSS_ROWS if dense else capacity
+    bf16 = jnp.bfloat16
+
+    def like(*shape):
+        return jax.ShapeDtypeStruct(shape, bf16)
+
+    def in_vmem(x):
+        return pltpu.with_memory_space_constraint(x, pltpu.VMEM)
+
+    gate, up = gate_weight.T, up_weight.T
+    both = [gate, swapped(gate, "expert", 0), up, swapped(up, "expert", 0)]
+    both += [down_weight, swapped(down_weight, "expert", 0)]
+    both = [in_vmem(w) for w in both]
+
+    total = width + LANES
+    payload = [like(rows, total)] * CHUNKS + ([like(tok_rows, tok_rows)] if dense else [])
+    payload = call(functools.partial(prepare_kernel, experts), payload, idx, tokens, routes, route_weights)
+
+    def pick(*blocks):
+        return call(
+            functools.partial(pick_kernel, experts, dense),
+            [like(own_rows, total), like(cross_rows, total), like(own_rows + cross_rows, rows)],
+            idx,
+            *blocks,
+            flops=2 * (own_rows + cross_rows) * rows * total,
+        )
+
+    def expert(own, cross):
+        count = own_rows + cross_rows
+        return call(
+            functools.partial(expert_kernel, experts),
+            [like(own_rows, width), like(cross_rows, width)],
+            idx,
+            own,
+            cross,
+            *both,
+            scratch=[pltpu.VMEM((2, count, half), bf16)],
+            flops=2 * 256 * half * 2 * width * 3,
+        )
+
+    def combine(made, *more, placed=False):
+        return call(
+            functools.partial(combine_kernel, placed),
+            [like(rows, width)],
+            idx,
+            *made,
+            *more,
+            flops=2 * (own_rows + cross_rows) * rows * width,
+        )[0]
+
+    outs = []
+    for q in range(CHUNKS):
+        x0 = payload[q]
+        x1 = exchange_outer(x0)
+        m1 = exchange_middle(x0)
+        o1 = move_out(m1)
+        m2 = exchange_middle(x1)
+        o2 = move_out(m2)
+        made = []
+        for blocks in ([x0], [x1], [m1, o1], [m2, o2]):
+            own, cross, chosen = pick(*blocks)
+            own, cross = expert(own, swapped(cross, "expert", 1))
+            made.append((chosen, own, swapped(cross, "expert", 1)))
+        p2 = combine(made[2])
+        s2 = exchange_middle(combine(made[2], move_in(p2)))
+        p3 = combine(made[3])
+        s3 = exchange_middle(combine(made[3], move_in(p3)))
+        s1 = exchange_outer(combine(made[1], s3))
+        outs.append(combine(made[0], s1, s2, placed=not dense))
+    if not dense:
+        return outs[0]
+    return call(place_kernel, [like(tok_rows, width)], idx, payload[-1], *outs)[0]
+
+
 def solution(mesh):
+    body = lined if mesh.shape["expert"] == 16 else dispatched
     return jax.shard_map(
-        shards,
+        body,
         mesh=mesh,
         in_specs=(
             P(("groups", "expert"), None),

time: 360 us -> 208 us (0.58)
  the two profiles are of different devices: /device:TPU:15 before, /device:TPU:0 now
where the time goes in v1:
time: 208 us
  waiting for transfers between devices  139 us (67%)
  Pallas kernels  37.8 us (18%)
  starting transfers between devices  23.1 us (11%)
  local copies, waits for them, and re-layouts  6.96 us (3%)
    ppermute x10, waiting for transfers between devices, along_line(): return lax.ppermute(x, 'expert', moves)  96.5 us
    ppermute x11, waiting for transfers between devices, swapped(): lax.ppermute(x, axis, [(i, i ^ 1 << apart) for i in range(lax.axis_size(a...  43 us
    pallas_call x15, Pallas kernels, call(): pl.pallas_call(kernel, out_shape=outs, in_specs=[pl.BlockSpec(memory_spac...  37.8 us
    ppermute x10, starting transfers between devices, along_line(): return lax.ppermute(x, 'expert', moves)  11.9 us
    ppermute x11, starting transfers between devices, swapped(): lax.ppermute(x, axis, [(i, i ^ 1 << apart) for i in range(lax.axis_size(a...  11.2 us
    unnamed x10, local copies, waits for them, and re-layouts  6.88 us
  transfers between devices with their start and end apart: 21, of which 10 were waited for; matrix products, arithmetic and copies ran while one was open for 0% of the time, Pallas kernels for 17%

profile of v1, /device:TPU:0, one launch (start us, length us, event | category | flops | bytes accessed | tf_op | source)
XLA Modules:
  0.0 207.7 jit_solution(13599528604846650301)
XLA Ops:
  1.7 1.2 copy-done.3
  3.7 3.1 %collective-permute-start.5 = (bf16[128,4224]{1,0:T(8,128)(2,1)S(1)}, bf16[128,4224]{1,0:T(8,128)(2,1)S(1)}, u32[]{:S(2)}, u32[]{:S(2)}) collective-permute-start(bf16[128,4224]{1,0:T(8,128)(2,1)S(1)} %shard_map.64.refs_0_), channel_id=1, source_target_pairs={{0,4},{1,5},{2,6},{3,7},{4,0},{5,1},{6,2},{7,3},{8,12},{9,13},{10,... | collective-permute-start | bytes 3244040 | tf_op jit(solution)/shard_map/ppermute | solution.py:73
  7.3 23.3 %collective-permute-done.5.refs_0_ = bf16[128,4224]{1,0:T(8,128)(2,1)S(1)} collective-permute-done((bf16[128,4224]{1,0:T(8,128)(2,1)S(1)}, bf16[128,4224]{1,0:T(8,128)(2,1)S(1)}, u32[]{:S(2)}, u32[]{:S(2)}) %collective-permute-start.5) | collective-permute-done | bytes 1081376 | tf_op jit(solution)/shard_map/ppermute | solution.py:73
  32.1 1.3 collective-permute-start.9
  33.4 1.3 collective-permute-start.16
  34.7 47.6 %collective-permute-done.9.refs_1_ = bf16[128,4224]{1,0:T(8,128)(2,1)S(1)} collective-permute-done((bf16[128,4224]{1,0:T(8,128)(2,1)S(1)}, bf16[128,4224]{1,0:T(8,128)(2,1)S(1)}, u32[]{:S(2)}, u32[]{:S(2)}) %collective-permute-start.9) | collective-permute-done | bytes 1081376 | tf_op jit(solution)/shard_map/ppermute | solution.py:73
  82.3 1.3 shard_map.69
  83.5 1.6 collective-permute-start.10
  85.1 20.3 %collective-permute-done.16.refs_1_ = bf16[128,4224]{1,0:T(8,128)(2,1)S(1)} collective-permute-done((bf16[128,4224]{1,0:T(8,128)(2,1)S(1)}, bf16[128,4224]{1,0:T(8,128)(2,1)S(1)}, u32[]{:S(2)}, u32[]{:S(2)}) %collective-permute-start.16) | collective-permute-done | bytes 1081376 | tf_op jit(solution)/shard_map/ppermute | solution.py:73
  105.5 1.3 shard_map.74
  106.7 1.6 collective-permute-start.17
  108.4 2.0 copy-done.1
  110.4 2.0 copy-done.2
  112.4 6.2 %shard_map.70 = (bf16[64,4096]{1,0:T(8,128)(2,1)S(1)}, bf16[64,4096]{1,0:T(8,128)(2,1)S(1)}) custom-call(s32[6]{0:T(128)S(1)} %stack.31.idx, bf16[64,4224]{1,0:T(8,128)(2,1)S(1)} %get-tuple-element.36.own, bf16[64,4224]{1,0:T(8,128)(2,1)S(1)} %collective-permute-done.10.cross, bf16[448,4096]{1,0:T(8,128)(2,1)S(1)} %bitcast.9, ...), custom_call_target="tpu_custom_call" | custom-call | flops 5637144576 | bytes 24150016 | tf_op jit(solution)/shard_map/pallas_call | solution.py:231
  119.2 10.4 %collective-permute-done.11.cross = bf16[64,4096]{1,0:T(8,128)(2,1)S(1)} collective-permute-done((bf16[64,4096]{1,0:T(8,128)(2,1)S(1)}, bf16[64,4096]{1,0:T(8,128)(2,1)S(1)}, u32[]{:S(2)}, u32[]{:S(2)}) %collective-permute-start.11) | collective-permute-done | bytes 524320 | tf_op jit(solution)/shard_map/ppermute | solution.py:16
  130.7 1.7 collective-permute-start.12
  132.4 6.2 %shard_map.75 = (bf16[64,4096]{1,0:T(8,128)(2,1)S(1)}, bf16[64,4096]{1,0:T(8,128)(2,1)S(1)}) custom-call(s32[6]{0:T(128)S(1)} %stack.31.idx, bf16[64,4224]{1,0:T(8,128)(2,1)S(1)} %get-tuple-element.41.own, bf16[64,4224]{1,0:T(8,128)(2,1)S(1)} %collective-permute-done.17.cross, bf16[448,4096]{1,0:T(8,128)(2,1)S(1)} %bitcast.10, ...), custom_call_target="tpu_custom_call" | custom-call | flops 5637144576 | bytes 24150016 | tf_op jit(solution)/shard_map/pallas_call | solution.py:231
  138.6 1.5 collective-permute-start.18
  140.2 1.2 shard_map.67
  142.1 1.2 shard_map.65
  143.3 1.5 collective-permute-start
  144.8 8.7 %collective-permute-done.18.cross = bf16[64,4096]{1,0:T(8,128)(2,1)S(1)} collective-permute-done((bf16[64,4096]{1,0:T(8,128)(2,1)S(1)}, bf16[64,4096]{1,0:T(8,128)(2,1)S(1)}, u32[]{:S(2)}, u32[]{:S(2)}) %collective-permute-start.18) | collective-permute-done | bytes 524320 | tf_op jit(solution)/shard_map/ppermute | solution.py:16
  154.6 1.4 collective-permute-start.19
  157.7 7.5 %collective-permute-done.6.cross = bf16[64,4224]{1,0:T(8,128)(2,1)S(1)} collective-permute-done((bf16[64,4224]{1,0:T(8,128)(2,1)S(1)}, bf16[64,4224]{1,0:T(8,128)(2,1)S(1)}, u32[]{:S(2)}, u32[]{:S(2)}) %collective-permute-start.6) | collective-permute-done | bytes 540704 | tf_op jit(solution)/shard_map/ppermute | solution.py:16
  165.2 6.2 %shard_map.68 = (bf16[64,4096]{1,0:T(8,128)(2,1)S(1)}, bf16[64,4096]{1,0:T(8,128)(2,1)S(1)}) custom-call(s32[6]{0:T(128)S(1)} %stack.31.idx, bf16[64,4224]{1,0:T(8,128)(2,1)S(1)} %get-tuple-element.31.own, bf16[64,4224]{1,0:T(8,128)(2,1)S(1)} %collective-permute-done.6.cross, bf16[448,4096]{1,0:T(8,128)(2,1)S(1)} %bitcast.11, ...), custom_call_target="tpu_custom_call" | custom-call | flops 5637144576 | bytes 24150016 | tf_op jit(solution)/shard_map/pallas_call | solution.py:231
  171.4 1.5 collective-permute-start.7
  175.4 8.2 %collective-permute-done.7.cross = bf16[64,4096]{1,0:T(8,128)(2,1)S(1)} collective-permute-done((bf16[64,4096]{1,0:T(8,128)(2,1)S(1)}, bf16[64,4096]{1,0:T(8,128)(2,1)S(1)}, u32[]{:S(2)}, u32[]{:S(2)}) %collective-permute-start.7) | collective-permute-done | bytes 524320 | tf_op jit(solution)/shard_map/ppermute | solution.py:16
  184.7 6.2 %shard_map.66 = (bf16[64,4096]{1,0:T(8,128)(2,1)S(1)}, bf16[64,4096]{1,0:T(8,128)(2,1)S(1)}) custom-call(s32[6]{0:T(128)S(1)} %stack.31.idx, bf16[64,4224]{1,0:T(8,128)(2,1)S(1)} %get-tuple-element.26.own, bf16[64,4224]{1,0:T(8,128)(2,1)S(1)} %collective-permute-done.cross, bf16[448,4096]{1,0:T(8,128)(2,1)S(1)} %bitcast.12, ...), custom_call_target="tpu_custom_call" | custom-call | flops 5637144576 | bytes 24150016 | tf_op jit(solution)/shard_map/pallas_call | solution.py:231
  191.0 1.8 collective-permute-start.4
  192.8 8.1 %collective-permute-done.4.cross = bf16[64,4096]{1,0:T(8,128)(2,1)S(1)} collective-permute-done((bf16[64,4096]{1,0:T(8,128)(2,1)S(1)}, bf16[64,4096]{1,0:T(8,128)(2,1)S(1)}, u32[]{:S(2)}, u32[]{:S(2)}) %collective-permute-start.4) | collective-permute-done | bytes 524320 | tf_op jit(solution)/shard_map/ppermute | solution.py:16
  200.9 4.6 %collective-permute-done.14.refs_0_ = bf16[128,4096]{1,0:T(8,128)(2,1)S(1)} collective-permute-done((bf16[128,4096]{1,0:T(8,128)(2,1)S(1)}, bf16[128,4096]{1,0:T(8,128)(2,1)S(1)}, u32[]{:S(2)}, u32[]{:S(2)}) %collective-permute-start.14) | collective-permute-done | bytes 1048608 | tf_op jit(solution)/shard_map/ppermute | solution.py:73
  205.6 2.1 %shard_map.78 = bf16[128,4096]{1,0:T(8,128)(2,1)} custom-call(s32[6]{0:T(128)S(1)} %stack.31.idx, bf16[128,128]{1,0:T(8,128)(2,1)S(1)} %get-tuple-element.25.pick, bf16[64,4096]{1,0:T(8,128)(2,1)S(1)} %get-tuple-element.28.own, bf16[64,4096]{1,0:T(8,128)(2,1)S(1)} %collective-permute-done.4.cross, bf16[128,4096]{1,0:T(8,128)(2,1)S(1)} %collective-permute-done.14.refs_0_, ...), custom_call_target="tpu_custom_call" | custom-call | flops 134217728 | bytes 4227072 | tf_op jit(solution)/shard_map/pallas_call | solution.py:231
  (36 shorter events, 12.9 us)
Async XLA Ops:
  1.7 1.2 copy-start.3
  2.9 105.5 %copy-start = (bf16[4096,448]{0,1:T(8,128)(2,1)S(1)}, bf16[4096,448]{0,1:T(8,128)(2,1)}, u32[]{:S(2)}) copy-start(bf16[4096,448]{0,1:T(8,128)(2,1)} %param.9) | copy-start | bytes 11010052
  3.7 26.9 %collective-permute-start.5 = (bf16[128,4224]{1,0:T(8,128)(2,1)S(1)}, bf16[128,4224]{1,0:T(8,128)(2,1)S(1)}, u32[]{:S(2)}, u32[]{:S(2)}) collective-permute-start(bf16[128,4224]{1,0:T(8,128)(2,1)S(1)} %shard_map.64.refs_0_), channel_id=1, source_target_pairs={{0,4},{1,5},{2,6},{3,7},{4,0},{5,1},{6,2},{7,3},{8,12},{9,13},{10,... | collective-permute-start | bytes 3244040 | tf_op jit(solution)/shard_map/ppermute | solution.py:73
  6.7 101.6 %collective-permute-start.1 = (bf16[448,4096]{1,0:T(8,128)(2,1)}, bf16[448,4096]{1,0:T(8,128)(2,1)S(1)}, u32[]{:S(2)}, u32[]{:S(2)}) collective-permute-start(bf16[448,4096]{1,0:T(8,128)(2,1)} %bitcast.8), channel_id=1, source_target_pairs={{0,1},{1,0},{2,3},{3,2},{4,5},{5,4},{6,7},{7,6},{8,9},{9,8},{10,11... | collective-permute-start | bytes 11010056 | tf_op jit(solution)/shard_map/ppermute | solution.py:16
  6.7 101.6 %collective-permute-start.2 = (bf16[448,4096]{1,0:T(8,128)(2,1)}, bf16[448,4096]{1,0:T(8,128)(2,1)S(1)}, u32[]{:S(2)}, u32[]{:S(2)}) collective-permute-start(bf16[448,4096]{1,0:T(8,128)(2,1)} %bitcast.13), channel_id=1, source_target_pairs={{0,1},{1,0},{2,3},{3,2},{4,5},{5,4},{6,7},{7,6},{8,9},{9,8},{10,11... | collective-permute-start | bytes 11010056 | tf_op jit(solution)/shard_map/ppermute | solution.py:16
  7.3 101.1 %collective-permute-start.3 = (bf16[896,2048]{1,0:T(8,128)(2,1)}, bf16[896,2048]{1,0:T(8,128)(2,1)S(1)}, u32[]{:S(2)}, u32[]{:S(2)}) collective-permute-start(bf16[896,2048]{1,0:T(8,128)(2,1)} %da.7), channel_id=1, source_target_pairs={{0,1},{1,0},{2,3},{3,2},{4,5},{5,4},{6,7},{7,6},{8,9},{9,8},{10,11... | collective-permute-start | bytes 11010056 | tf_op jit(solution)/shard_map/ppermute | solution.py:16
  30.6 1.5 collective-permute-start.8
  31.3 2.1 collective-permute-start.15
  32.1 50.2 %collective-permute-start.9 = (bf16[128,4224]{1,0:T(8,128)(2,1)S(1)}, bf16[128,4224]{1,0:T(8,128)(2,1)S(1)}, u32[]{:S(2)}, u32[]{:S(2)}) collective-permute-start(bf16[128,4224]{1,0:T(8,128)(2,1)S(1)} %collective-permute-done.8.refs_0_), channel_id=1, source_target_pairs={{4,0},{5,1},{6,2},{7,3},{8,12},{9,13},{10,14},{11,15},{20,16},{21,... | collective-permute-start | bytes 3244040 | tf_op jit(solution)/shard_map/ppermute | solution.py:73
  33.4 72.1 %collective-permute-start.16 = (bf16[128,4224]{1,0:T(8,128)(2,1)S(1)}, bf16[128,4224]{1,0:T(8,128)(2,1)S(1)}, u32[]{:S(2)}, u32[]{:S(2)}) collective-permute-start(bf16[128,4224]{1,0:T(8,128)(2,1)S(1)} %collective-permute-done.15.refs_0_), channel_id=1, source_target_pairs={{4,0},{5,1},{6,2},{7,3},{8,12},{9,13},{10,14},{11,15},{20,16},{21,... | collective-permute-start | bytes 3244040 | tf_op jit(solution)/shard_map/ppermute | solution.py:73
  83.5 24.8 %collective-permute-start.10 = (bf16[64,4224]{1,0:T(8,128)(2,1)S(1)}, bf16[64,4224]{1,0:T(8,128)(2,1)S(1)}, u32[]{:S(2)}, u32[]{:S(2)}) collective-permute-start(bf16[64,4224]{1,0:T(8,128)(2,1)S(1)} %get-tuple-element.37), channel_id=1, source_target_pairs={{0,2},{1,3},{2,0},{3,1},{4,6},{5,7},{6,4},{7,5},{8,10},{9,11},{10,... | collective-permute-start | bytes 1622024 | tf_op jit(solution)/shard_map/ppermute | solution.py:16
  106.7 25.7 %collective-permute-start.17 = (bf16[64,4224]{1,0:T(8,128)(2,1)S(1)}, bf16[64,4224]{1,0:T(8,128)(2,1)S(1)}, u32[]{:S(2)}, u32[]{:S(2)}) collective-permute-start(bf16[64,4224]{1,0:T(8,128)(2,1)S(1)} %get-tuple-element.42), channel_id=1, source_target_pairs={{0,2},{1,3},{2,0},{3,1},{4,6},{5,7},{6,4},{7,5},{8,10},{9,11},{10,... | collective-permute-start | bytes 1622024 | tf_op jit(solution)/shard_map/ppermute | solution.py:16
  108.3 2.0 copy-start.1
  110.4 2.0 copy-start.2
  118.7 11.0 %collective-permute-start.11 = (bf16[64,4096]{1,0:T(8,128)(2,1)S(1)}, bf16[64,4096]{1,0:T(8,128)(2,1)S(1)}, u32[]{:S(2)}, u32[]{:S(2)}) collective-permute-start(bf16[64,4096]{1,0:T(8,128)(2,1)S(1)} %get-tuple-element.39), channel_id=1, source_target_pairs={{0,2},{1,3},{2,0},{3,1},{4,6},{5,7},{6,4},{7,5},{8,10},{9,11},{10,... | collective-permute-start | bytes 1572872 | tf_op jit(solution)/shard_map/ppermute | solution.py:16
  130.7 25.3 %collective-permute-start.12 = (bf16[128,4096]{1,0:T(8,128)(2,1)S(1)}, bf16[128,4096]{1,0:T(8,128)(2,1)S(1)}, u32[]{:S(2)}, u32[]{:S(2)}) collective-permute-start(bf16[128,4096]{1,0:T(8,128)(2,1)S(1)} %shard_map.71), channel_id=1, source_target_pairs={{0,4},{1,5},{2,6},{3,7},{12,8},{13,9},{14,10},{15,11},{16,20},{17,... | collective-permute-start | bytes 3145736 | tf_op jit(solution)/shard_map/ppermute | solution.py:73
  138.6 14.9 %collective-permute-start.18 = (bf16[64,4096]{1,0:T(8,128)(2,1)S(1)}, bf16[64,4096]{1,0:T(8,128)(2,1)S(1)}, u32[]{:S(2)}, u32[]{:S(2)}) collective-permute-start(bf16[64,4096]{1,0:T(8,128)(2,1)S(1)} %get-tuple-element.44), channel_id=1, source_target_pairs={{0,2},{1,3},{2,0},{3,1},{4,6},{5,7},{6,4},{7,5},{8,10},{9,11},{10,... | collective-permute-start | bytes 1572872 | tf_op jit(solution)/shard_map/ppermute | solution.py:16
  141.4 23.7 %collective-permute-start.6 = (bf16[64,4224]{1,0:T(8,128)(2,1)S(1)}, bf16[64,4224]{1,0:T(8,128)(2,1)S(1)}, u32[]{:S(2)}, u32[]{:S(2)}) collective-permute-start(bf16[64,4224]{1,0:T(8,128)(2,1)S(1)} %get-tuple-element.32), channel_id=1, source_target_pairs={{0,2},{1,3},{2,0},{3,1},{4,6},{5,7},{6,4},{7,5},{8,10},{9,11},{10,... | collective-permute-start | bytes 1622024 | tf_op jit(solution)/shard_map/ppermute | solution.py:16
  143.3 41.4 %collective-permute-start = (bf16[64,4224]{1,0:T(8,128)(2,1)S(1)}, bf16[64,4224]{1,0:T(8,128)(2,1)S(1)}, u32[]{:S(2)}, u32[]{:S(2)}) collective-permute-start(bf16[64,4224]{1,0:T(8,128)(2,1)S(1)} %get-tuple-element.27), channel_id=1, source_target_pairs={{0,2},{1,3},{2,0},{3,1},{4,6},{5,7},{6,4},{7,5},{8,10},{9,11},{10,... | collective-permute-start | bytes 1622024 | tf_op jit(solution)/shard_map/ppermute | solution.py:16
  154.6 18.9 %collective-permute-start.19 = (bf16[128,4096]{1,0:T(8,128)(2,1)S(1)}, bf16[128,4096]{1,0:T(8,128)(2,1)S(1)}, u32[]{:S(2)}, u32[]{:S(2)}) collective-permute-start(bf16[128,4096]{1,0:T(8,128)(2,1)S(1)} %shard_map.76), channel_id=1, source_target_pairs={{0,4},{1,5},{2,6},{3,7},{12,8},{13,9},{14,10},{15,11},{16,20},{17,... | collective-permute-start | bytes 3145736 | tf_op jit(solution)/shard_map/ppermute | solution.py:73
  157.0 26.7 %collective-permute-start.13 = (bf16[128,4096]{1,0:T(8,128)(2,1)S(1)}, bf16[128,4096]{1,0:T(8,128)(2,1)S(1)}, u32[]{:S(2)}, u32[]{:S(2)}) collective-permute-start(bf16[128,4096]{1,0:T(8,128)(2,1)S(1)} %shard_map.72), channel_id=1, source_target_pairs={{4,8},{5,9},{6,10},{7,11},{8,4},{9,5},{10,6},{11,7},{20,24},{21,25... | collective-permute-start | bytes 3145736 | tf_op jit(solution)/shard_map/ppermute | solution.py:73
  171.4 12.2 %collective-permute-start.7 = (bf16[64,4096]{1,0:T(8,128)(2,1)S(1)}, bf16[64,4096]{1,0:T(8,128)(2,1)S(1)}, u32[]{:S(2)}, u32[]{:S(2)}) collective-permute-start(bf16[64,4096]{1,0:T(8,128)(2,1)S(1)} %get-tuple-element.34), channel_id=1, source_target_pairs={{0,2},{1,3},{2,0},{3,1},{4,6},{5,7},{6,4},{7,5},{8,10},{9,11},{10,... | collective-permute-start | bytes 1572872 | tf_op jit(solution)/shard_map/ppermute | solution.py:16
  174.5 26.5 %collective-permute-start.20 = (bf16[128,4096]{1,0:T(8,128)(2,1)S(1)}, bf16[128,4096]{1,0:T(8,128)(2,1)S(1)}, u32[]{:S(2)}, u32[]{:S(2)}) collective-permute-start(bf16[128,4096]{1,0:T(8,128)(2,1)S(1)} %shard_map.77), channel_id=1, source_target_pairs={{4,8},{5,9},{6,10},{7,11},{8,4},{9,5},{10,6},{11,7},{20,24},{21,25... | collective-permute-start | bytes 3145736 | tf_op jit(solution)/shard_map/ppermute | solution.py:73
  184.7 20.9 %collective-permute-start.14 = (bf16[128,4096]{1,0:T(8,128)(2,1)S(1)}, bf16[128,4096]{1,0:T(8,128)(2,1)S(1)}, u32[]{:S(2)}, u32[]{:S(2)}) collective-permute-start(bf16[128,4096]{1,0:T(8,128)(2,1)S(1)} %shard_map.73), channel_id=1, source_target_pairs={{0,4},{1,5},{2,6},{3,7},{4,0},{5,1},{6,2},{7,3},{8,12},{9,13},{10,... | collective-permute-start | bytes 3145736 | tf_op jit(solution)/shard_map/ppermute | solution.py:73
  191.0 9.9 %collective-permute-start.4 = (bf16[64,4096]{1,0:T(8,128)(2,1)S(1)}, bf16[64,4096]{1,0:T(8,128)(2,1)S(1)}, u32[]{:S(2)}, u32[]{:S(2)}) collective-permute-start(bf16[64,4096]{1,0:T(8,128)(2,1)S(1)} %get-tuple-element.29), channel_id=1, source_target_pairs={{0,2},{1,3},{2,0},{3,1},{4,6},{5,7},{6,4},{7,5},{8,10},{9,11},{10,... | collective-permute-start | bytes 1572872 | tf_op jit(solution)/shard_map/ppermute | solution.py:16
